TPU v7x, 32 devices: a whole 2x2x4 slice. The times are simulated.
32 devices in a mesh: groups: 2 (over y), particle: 4 (over z), cuts: 2 (over x), sub: 2 (over core).
Axes of the slice: x: 2, y: 2, z: 4, core: 2. Of those that a mesh axis runs over, the one named last changes fastest.
Arguments:
- weights: float32 [32, 512, 512], P(('groups', 'particle', 'cuts', 'sub')), parts along dimension 0, may hold values from -32 to 32, as said below
- features: float32 [2048, 512], P('groups'), parts along dimension 0, may hold values from -0.25 to 0.25
- targets: float32 [2048, 512], P('groups'), parts along dimension 0, may hold values from -6 to 6
Outputs:
- update: float32 [32, 512, 512], P(('groups', 'particle', 'cuts', 'sub')), parts along dimension 0
There are 2 independent parts, one for each index of `groups`. A program takes and returns all parts, laid end to end along the dimension named above; each array names one. Nothing has to cross between parts.
Inputs may be any that keep to these rules, and one draw needn't show every extreme that they name: `weights`: parameters of every particle are of order one.
All inputs are finite; a program needn't handle non-finite values.
Results may differ from a plain program's by a relative error of at most 0.000068.
Values sent between devices are 32-bit elements; how exact they have to be, the bound alone decides.
A program may use at most 64 MiB of HBM per device.

v0:
```python
import math

import jax
import jax.numpy as jnp
from jax import lax
from jax.sharding import PartitionSpec as P

epsilon = 1e-06


def posterior_grad(params, features, targets):
    highest = lax.Precision.HIGHEST
    misfit = targets - jnp.dot(features, params, precision=highest)
    product = lax.dot_general(features, misfit, (((0,), (0,)), ((), ())), precision=highest)
    return product - params


def kernel_weights(slab, count, width):
    highest = lax.Precision.HIGHEST
    partial_value = jnp.dot(slab, slab.T, precision=highest)
    gram = lax.psum(partial_value, ("particle", "cuts", "sub"))
    diagonal = jnp.diagonal(gram)
    mean_sq = (diagonal[:, None] + diagonal[None, :] - 2.0 * gram) / width
    scale = jnp.sum(mean_sq) / (count * (count - 1)) + epsilon
    kernel_mat = jnp.exp(-math.log(count) * mean_sq / scale)
    return (kernel_mat, scale)


def on_device(weights, features, targets):
    highest = lax.Precision.HIGHEST
    outer = lax.axis_size("particle") * lax.axis_size("cuts")
    inner = lax.axis_size("sub")
    count = outer * inner
    width = weights.shape[1] * weights.shape[2]
    piece = width // count
    sectioned = weights.reshape(1, outer, inner, piece)
    grads = posterior_grad(weights[0], features, targets)
    grad_sectioned = grads.reshape(1, outer, inner, piece)
    param_slab, grad_slab = (
        lax.all_to_all(
            lax.all_to_all(
                sectioned, ("particle", "cuts"), split_axis=1, concat_axis=0, tiled=True
            ),
            "sub",
            split_axis=2,
            concat_axis=1,
            tiled=True,
        ),
        lax.all_to_all(
            lax.all_to_all(
                grad_sectioned, ("particle", "cuts"), split_axis=1, concat_axis=0, tiled=True
            ),
            "sub",
            split_axis=2,
            concat_axis=1,
            tiled=True,
        ),
    )
    param_slab = param_slab.reshape(count, piece)
    grad_slab = grad_slab.reshape(count, piece)
    kernel_mat, scale = kernel_weights(param_slab, count, width)
    row_total = jnp.sum(kernel_mat, axis=1)[:, None]
    drive = jnp.dot(kernel_mat, grad_slab, precision=highest)
    pull = jnp.dot(kernel_mat, param_slab, precision=highest)
    result = (drive + (row_total * param_slab - pull) / scale) / row_total
    back_sectioned = result.reshape(outer, inner, 1, 1, piece)
    returned = lax.all_to_all(
        lax.all_to_all(
            back_sectioned, ("particle", "cuts"), split_axis=0, concat_axis=2, tiled=True
        ),
        "sub",
        split_axis=1,
        concat_axis=3,
        tiled=True,
    )
    return returned.reshape(weights.shape)


def solution(mesh):
    placed = (
        P(("groups", "particle", "cuts", "sub"), None, None),
        P("groups", None),
        P("groups", None),
    )
    return jax.shard_map(
        on_device,
        mesh=mesh,
        in_specs=placed,
        out_specs=P(("groups", "particle", "cuts", "sub"), None, None),
        check_vma=False,
    )
```

profile of v0, /device:TPU:0, one launch (start us, length us, event | category | flops | bytes accessed | tf_op | source)
XLA Modules:
  0.0 172.3 jit_solution(5891310846580032677)
XLA Ops:
  0.0 0.0 copy-start
  0.0 0.0 copy-start.1
  0.0 2.7 %copy.17 = f32[1,512,512]{1,2,0:T(8,128)} copy(f32[1,512,512]{2,1,0:T(8,128)} %param.3) | data formatting | bytes 2097152 | tf_op args[0]
  2.7 0.0 copy-done
  2.7 0.0 copy-done.1
  2.7 0.0 copy-start.2
  2.7 0.0 copy-start.3
  2.7 3.4 %fusion.11 = f32[1024,512]{1,0:T(8,128)S(1)} fusion(f32[1024,512]{1,0:T(8,128)S(1)} %copy-done, f32[1,512,512]{2,1,0:T(8,128)S(1)} %copy-done.1), kind=kOutput, calls=%fused_computation.9 | convolution fusion | flops 3221225472 | bytes 5242880 | tf_op jit(solution)/shard_map/dot_general | solution.py:13
  6.1 0.0 copy-done.2
  6.2 0.0 copy-done.3
  6.2 4.6 %fusion.8 = f32[512,512]{0,1:T(8,128)} fusion(f32[1024,512]{1,0:T(8,128)S(1)} %copy-done, f32[1024,512]{1,0:T(8,128)S(1)} %copy-done.3, f32[1024,512]{1,0:T(8,128)S(1)} %fusion.11, f32[1,512,512]{1,2,0:T(8,128)S(1)} %copy-done.2), kind=kOutput, calls=%fused_computation.8 | convolution fusion | flops 3222011904 | bytes 8388608 | tf_op jit(solution)/shard_map/dot_general | solution.py:14
  10.7 2.5 %copy.18 = f32[512,512]{1,0:T(8,128)} copy(f32[512,512]{0,1:T(8,128)} %fusion.8) | data formatting | bytes 2097152 | tf_op jit(solution)/shard_map/sub | solution.py:15
  13.3 3.1 %reshape.38 = f32[1,8,2,16384]{3,2,1,0:T(2,128)} reshape(f32[512,512]{1,0:T(8,128)} %copy.18) | data formatting | bytes 2097152 | tf_op jit(solution)/shard_map/reshape | solution.py:38
  16.4 7.3 %all-to-all-start.2 = ((f32[1,8,2,16384]{3,2,0,1:T(2,128)}), f32[1,8,2,16384]{3,2,0,1:T(2,128)}, u32[]{:S(2)}, u32[]{:S(2)}) async-start(f32[1,8,2,16384]{3,2,0,1:T(2,128)} %bitcast.36), calls=%async_computation.2 | async-start | bytes 2097152 | tf_op jit(solution)/shard_map/all_to_all | solution.py:50
  23.6 1.9 %reshape.36 = f32[1,8,2,16384]{3,2,0,1:T(2,128)} reshape(f32[1,512,512]{2,1,0:T(8,128)S(1)} %copy-done.1) | data formatting | bytes 2097152 | tf_op jit(solution)/shard_map/reshape | solution.py:36
  25.5 24.0 %all-to-all-done.2 = f32[1,8,2,16384]{3,2,0,1:T(2,128)} async-done(((f32[1,8,2,16384]{3,2,0,1:T(2,128)}), f32[1,8,2,16384]{3,2,0,1:T(2,128)}, u32[]{:S(2)}, u32[]{:S(2)}) %all-to-all-start.2) | async-done | bytes 1048608 | tf_op jit(solution)/shard_map/all_to_all | solution.py:50
  49.5 1.8 %copy.20 = f32[8,1,2,16384]{3,0,1,2:T(8,128)S(1)} copy(f32[8,1,2,16384]{3,2,0,1:T(2,128)} %bitcast.5) | data formatting | bytes 2097152 | tf_op jit(solution)/shard_map/all_to_all | solution.py:50
  51.3 5.4 %all_to_all.75 = f32[8,1,2,16384]{3,0,1,2:T(8,128)} all-to-all(f32[8,1,2,16384]{3,0,1,2:T(8,128)S(1)} %copy.20), channel_id=1, replica_groups=mesh['groups'=2,'particle'=4,'cuts'=2,'sub'=2] {'sub'}, dimensions={2} | all-to-all | bytes 2097152 | tf_op jit(solution)/shard_map/all_to_all | solution.py:49
  56.7 3.7 %all-to-all-start = ((f32[1,8,2,16384]{3,2,0,1:T(2,128)}), f32[1,8,2,16384]{3,2,0,1:T(2,128)S(1)}, u32[]{:S(2)}, u32[]{:S(2)}) async-start(f32[1,8,2,16384]{3,2,0,1:T(2,128)} %reshape.36), calls=%async_computation | async-start | bytes 2097152 | tf_op jit(solution)/shard_map/all_to_all | solution.py:41
  60.5 3.0 %copy.21 = f32[8,1,2,16384]{3,2,0,1:T(2,128)} copy(f32[8,1,2,16384]{3,0,1,2:T(8,128)} %all_to_all.75) | data formatting | bytes 2097152 | tf_op jit(solution)/shard_map/all_to_all | solution.py:49
  63.5 3.0 %reshape.39 = f32[16,16384]{1,0:T(8,128)} reshape(f32[8,1,2,16384]{3,2,0,1:T(2,128)} %copy.21) | data formatting | bytes 2097152 | tf_op jit(solution)/shard_map/reshape | solution.py:60
  66.5 20.1 %all-to-all-done = f32[1,8,2,16384]{3,2,0,1:T(2,128)S(1)} async-done(((f32[1,8,2,16384]{3,2,0,1:T(2,128)}), f32[1,8,2,16384]{3,2,0,1:T(2,128)S(1)}, u32[]{:S(2)}, u32[]{:S(2)}) %all-to-all-start) | async-done | bytes 1048608 | tf_op jit(solution)/shard_map/all_to_all | solution.py:41
  86.6 0.6 copy.15
  87.2 4.6 %all_to_all.76 = f32[8,1,2,16384]{3,0,1,2:T(8,128)S(1)} all-to-all(f32[8,1,2,16384]{3,0,1,2:T(8,128)S(1)} %copy.15), channel_id=1, replica_groups=mesh['groups'=2,'particle'=4,'cuts'=2,'sub'=2] {'sub'}, dimensions={2} | all-to-all | bytes 2097152 | tf_op jit(solution)/shard_map/all_to_all | solution.py:40
  91.8 1.8 %copy.16 = f32[8,1,2,16384]{3,2,0,1:T(2,128)} copy(f32[8,1,2,16384]{3,0,1,2:T(8,128)S(1)} %all_to_all.76) | data formatting | bytes 2097152 | tf_op jit(solution)/shard_map/all_to_all | solution.py:40
  93.5 1.9 %reshape.37 = f32[16,16384]{1,0:T(8,128)S(1)} reshape(f32[8,1,2,16384]{3,2,0,1:T(2,128)} %copy.16) | data formatting | bytes 2097152 | tf_op jit(solution)/shard_map/reshape | solution.py:59
  95.5 1.5 fusion.15
  97.0 32.1 %psum.7 = f32[16,16]{1,0:T(8,128)S(1)} all-reduce(f32[16,16]{1,0:T(8,128)S(1)} %fusion.15), channel_id=1, replica_groups=mesh['groups'=2,'particle'=4,'cuts'=2,'sub'=2] {'particle','cuts','sub'}, use_global_device_ids=true, to_apply=%region_0.0 | all-reduce | flops 256 | bytes 2048 | tf_op jit(solution)/shard_map/psum | solution.py:21
  129.1 0.7 gather_fusion
  129.8 0.7 multiply_reduce_fusion
  131.1 0.2 fusion.13
  131.3 2.3 %fusion.14 = f32[16,16384]{1,0:T(8,128)S(1)} fusion(f32[16,16384]{1,0:T(8,128)} %reshape.39, f32[16,16]{1,0:T(8,128)S(1)} %psum.7, f32[]{:T(128)S(6)} %add.28, f32[16]{0:T(128)S(1)} %gather_fusion), kind=kOutput, calls=%fused_computation.16 | convolution fusion | flops 50332928 | bytes 2098244 | tf_op jit(solution)/shard_map/dot_general | solution.py:63
  133.6 2.1 %fusion.2 = f32[16,16384]{1,0:T(8,128)} fusion(f32[16,16384]{1,0:T(8,128)S(1)} %fusion.14, f32[16,16384]{1,0:T(8,128)S(1)} %reshape.37, f32[]{:T(128)S(6)} %add.28, f32[16]{0:T(128)S(1)} %fusion.13, f32[16,16]{1,0:T(8,128)S(1)} %psum.7, f32[16]{0:T(128)S(1)} %gather_fusion), kind=kOutput, calls=%fused_computation.4 | convolution fusion | flops 51643648 | bytes 3146884 | tf_op jit(solution)/shard_map/dot_general | solution.py:64
  135.7 1.8 %reshape.40 = f32[8,2,1,1,16384]{4,1,0,3,2:T(2,128)S(1)} reshape(f32[16,16384]{1,0:T(8,128)} %fusion.2) | data formatting | bytes 2097152 | tf_op jit(solution)/shard_map/reshape | solution.py:66
  137.5 26.9 %all_to_all.77 = f32[8,2,1,1,16384]{4,1,3,2,0:T(2,128)S(1)} all-to-all(f32[8,2,1,1,16384]{4,1,3,2,0:T(2,128)S(1)} %bitcast.37), channel_id=1, replica_groups=mesh['groups'=2,'particle'=4,'cuts'=2,'sub'=2] {'particle','cuts'}, dimensions={0} | all-to-all | bytes 2097152 | tf_op jit(solution)/shard_map/all_to_all | solution.py:68
  164.4 0.6 copy.23
  165.0 4.6 %all_to_all.78 = f32[1,2,8,1,16384]{4,2,3,0,1:T(8,128)S(1)} all-to-all(f32[1,2,8,1,16384]{4,2,3,0,1:T(8,128)S(1)} %copy.23), channel_id=1, replica_groups=mesh['groups'=2,'particle'=4,'cuts'=2,'sub'=2] {'sub'}, dimensions={1} | all-to-all | bytes 2097152 | tf_op jit(solution)/shard_map/all_to_all | solution.py:67
  169.6 0.8 copy.24
  170.4 1.9 %reshape.41 = f32[1,512,512]{2,1,0:T(8,128)} reshape(f32[1,1,8,2,1,16384]{5,3,2,4,1,0:T(2,128)S(1)} %copy.24) | data formatting | bytes 2097152 | tf_op jit(solution)/shard_map/reshape | solution.py:76
  (1 shorter events, 0.0 us)
Async XLA Ops:
  0.0 2.7 %copy-start = (f32[1024,512]{1,0:T(8,128)S(1)}, f32[1024,512]{1,0:T(8,128)}, u32[]{:S(2)}) copy-start(f32[1024,512]{1,0:T(8,128)} %param.4) | copy-start | bytes 6291460
  0.0 2.7 %copy-start.1 = (f32[1,512,512]{2,1,0:T(8,128)S(1)}, f32[1,512,512]{2,1,0:T(8,128)}, u32[]{:S(2)}) copy-start(f32[1,512,512]{2,1,0:T(8,128)} %param.3) | copy-start | bytes 3145732
  2.7 3.5 %copy-start.2 = (f32[1,512,512]{1,2,0:T(8,128)S(1)}, f32[1,512,512]{1,2,0:T(8,128)}, u32[]{:S(2)}) copy-start(f32[1,512,512]{1,2,0:T(8,128)} %copy.17) | copy-start | bytes 3145732
  2.7 3.5 %copy-start.3 = (f32[1024,512]{1,0:T(8,128)S(1)}, f32[1024,512]{1,0:T(8,128)}, u32[]{:S(2)}) copy-start(f32[1024,512]{1,0:T(8,128)} %param.5) | copy-start | bytes 6291460
  16.4 33.1 %all-to-all-start.2 = ((f32[1,8,2,16384]{3,2,0,1:T(2,128)}), f32[1,8,2,16384]{3,2,0,1:T(2,128)}, u32[]{:S(2)}, u32[]{:S(2)}) async-start(f32[1,8,2,16384]{3,2,0,1:T(2,128)} %bitcast.36), calls=%async_computation.2 | async-start | bytes 2097152 | tf_op jit(solution)/shard_map/all_to_all | solution.py:50
  56.7 29.8 %all-to-all-start = ((f32[1,8,2,16384]{3,2,0,1:T(2,128)}), f32[1,8,2,16384]{3,2,0,1:T(2,128)S(1)}, u32[]{:S(2)}, u32[]{:S(2)}) async-start(f32[1,8,2,16384]{3,2,0,1:T(2,128)} %reshape.36), calls=%async_computation | async-start | bytes 2097152 | tf_op jit(solution)/shard_map/all_to_all | solution.py:41
where the time goes:
time: 173 us; the launch traced here: 172 us
  blocking collectives  73.5 us (42%)
  waiting for transfers between devices  44.1 us (25%)
  local copies, waits for them, and re-layouts  28.2 us (16%)
  matrix products  13.9 us (8%)
  starting transfers between devices  11 us (6%)
    psum x1, blocking collectives, kernel_weights(): gram = lax.psum(partial_value, ('particle', 'cuts', 'sub'))  32.1 us
    all_to_all x1, blocking collectives, on_device(): lax.all_to_all(back_sectioned, ('particle', 'cuts'), split_axis=0, concat...  26.9 us
    all_to_all x1, waiting for transfers between devices, on_device(): lax.all_to_all(grad_sectioned, ('particle', 'cuts'), split_axis=1, concat...  24 us
    all_to_all x1, waiting for transfers between devices, on_device(): lax.all_to_all(sectioned, ('particle', 'cuts'), split_axis=1, concat_axis...  20.1 us
    all_to_all x1, starting transfers between devices, on_device(): lax.all_to_all(grad_sectioned, ('particle', 'cuts'), split_axis=1, concat...  7.26 us
    all_to_all x1, blocking collectives, on_device(): lax.all_to_all(lax.all_to_all(grad_sectioned, ('particle', 'cuts'), split...  5.39 us
    dot_general x1, matrix products, posterior_grad(): lax.dot_general(features, misfit, (((0,), (0,)), ((), ())), precision=hig...  4.58 us
    all_to_all x1, blocking collectives, on_device(): lax.all_to_all(lax.all_to_all(sectioned, ('particle', 'cuts'), split_axis...  4.58 us
  transfers between devices with their start and end apart: 2, of which 2 were waited for; matrix products, arithmetic and copies ran while one was open for 5% of the time, Pallas kernels for 0%

commit v1 on v0

v1 whole, which is shorter than its diff:
```python
import functools
import math

import jax
import jax.numpy as jnp
from jax import lax
from jax.experimental import pallas as pl
from jax.experimental.pallas import tpu as pltpu
from jax.sharding import PartitionSpec as P

epsilon = 1e-06
HIGHEST = lax.Precision.HIGHEST
AXES = ("particle", "cuts", "sub")
PARTS = 2


def dot(a, b, contract=((1,), (0,))):
    return lax.dot_general(
        a, b, (contract, ((), ())), precision=HIGHEST, preferred_element_type=jnp.float32
    )


def kernel_weights(gram, count, width):
    row = lax.broadcasted_iota(jnp.int32, gram.shape, 0)
    col = lax.broadcasted_iota(jnp.int32, gram.shape, 1)
    diagonal = jnp.where(row == col, gram, 0.0)
    own = jnp.sum(diagonal, axis=1, keepdims=True)
    other = jnp.sum(diagonal, axis=0, keepdims=True)
    mean_sq = jnp.where(col < count, (own + other - 2.0 * gram) / width, 0.0)
    scale = jnp.sum(mean_sq, keepdims=True) / (count * (count - 1)) + epsilon
    kernel_mat = jnp.where(col < count, jnp.exp(-math.log(count) * mean_sq / scale), 0.0)
    return kernel_mat / jnp.sum(kernel_mat, axis=1, keepdims=True), scale


def body(sizes, w_hbm, x_hbm, t_hbm, out_hbm,
         w_v, x_v, t_v, slab, mixed, p_v, gram_own, gram_all, second, cross, out_v,
         local_sem, out_sem, send_w, recv_w, send_g, recv_g, send_p, recv_p):
    n_particle, n_cuts, n_sub = sizes
    count = n_particle * n_cuts * n_sub
    feats, beams = w_hbm.shape
    half = feats // PARTS
    rows = half // count
    group = lax.axis_index("groups")
    mine = [lax.axis_index(name) for name in AXES]
    me = (mine[0] * n_cuts + mine[1]) * n_sub + mine[2]

    def peer(k):
        k = count - 1 - k
        z = lax.rem(mine[0] + k // (n_cuts * n_sub), n_particle)
        x = lax.rem(mine[1] + lax.rem(k // n_sub, n_cuts), n_cuts)
        c = lax.rem(mine[2] + lax.rem(k, n_sub), n_sub)
        return (group, z, x, c), (z * n_cuts + x) * n_sub + c

    def each_peer(step):
        def go(k, carry):
            step(*peer(k))
            return carry
        lax.fori_loop(0, count - 1, go, 0)

    def place(part, index):
        return pl.ds(pl.multiple_of(part * half + index * rows, rows), rows)

    def block(index):
        return pl.ds(pl.multiple_of(index * rows, rows), rows)

    def copy_w(part, device, to, frm):
        return pltpu.make_async_remote_copy(
            src_ref=w_hbm.at[place(part, to)], dst_ref=slab.at[part, block(frm)],
            send_sem=send_w.at[part, to], recv_sem=recv_w.at[part, frm],
            device_id=device, device_id_type=pl.DeviceIdType.MESH)

    def copy_g(device, to, frm):
        return pltpu.make_async_remote_copy(
            src_ref=gram_own, dst_ref=gram_all.at[frm],
            send_sem=send_g.at[to], recv_sem=recv_g.at[frm],
            device_id=device, device_id_type=pl.DeviceIdType.MESH)

    def copy_p(part, device, to, frm):
        return pltpu.make_async_remote_copy(
            src_ref=mixed.at[part, block(to)], dst_ref=p_v.at[place(part, frm)],
            send_sem=send_p.at[part, to], recv_sem=recv_p.at[part, frm],
            device_id=device, device_id_type=pl.DeviceIdType.MESH)

    barrier = pltpu.get_barrier_semaphore()
    each_peer(lambda device, index: pl.semaphore_signal(
        barrier, inc=1, device_id=device, device_id_type=pl.DeviceIdType.MESH))
    loads = [
        pltpu.make_async_copy(x_hbm, x_v, local_sem.at[0]),
        pltpu.make_async_copy(t_hbm, t_v, local_sem.at[1]),
        pltpu.make_async_copy(w_hbm, w_v, local_sem.at[2]),
    ]
    own = [
        pltpu.make_async_copy(w_hbm.at[place(part, me)], slab.at[part, block(me)], local_sem.at[3 + part])
        for part in range(PARTS)
    ]
    for copy in loads + own:
        copy.start()
    pl.semaphore_wait(barrier, count - 1)
    for part in range(PARTS):
        each_peer(lambda device, index: copy_w(part, device, index, me).start())

    loads[0].wait()
    loads[1].wait()
    tile = 128

    def moments(step, carry):
        at = pl.ds(pl.multiple_of(step * tile, tile), tile)
        left = x_v[:, at]
        second[at, :] = dot(left, x_v[...], ((0,), (0,)))
        cross[at, :] = dot(left, t_v[...], ((0,), (0,)))
        return carry
    lax.fori_loop(0, feats // tile, moments, 0)

    total = jnp.zeros((half, half), jnp.float32)
    for part in range(PARTS):
        own[part].wait()
        each_peer(lambda device, index: copy_w(part, device, me, index).wait_recv())
        held = slab[part]
        total = total + dot(held, held, ((1,), (1,)))
    same = (
        lax.rem(lax.broadcasted_iota(jnp.int32, (half, half), 0), rows)
        == lax.rem(lax.broadcasted_iota(jnp.int32, (half, half), 1), rows)
    )
    lanes = gram_own.shape[1]
    total = jnp.where(same, total, 0.0).reshape(count, rows, half)
    pick = (
        lax.broadcasted_iota(jnp.int32, (half, lanes), 0) // rows
        == lax.broadcasted_iota(jnp.int32, (half, lanes), 1)
    ).astype(jnp.float32)
    gram_own[...] = dot(jnp.sum(total, axis=1), pick)
    each_peer(lambda device, index: copy_g(device, index, me).start())
    gram_all[pl.ds(me, 1)] = gram_own[...][None]
    each_peer(lambda device, index: copy_g(device, me, index).wait_recv())
    gram = jnp.sum(gram_all[...], axis=0)
    normal, scale = kernel_weights(gram, count, feats * beams)
    spread = dot(normal, pick, ((1,), (1,)))
    spread = jnp.broadcast_to(spread[:, None, :], (count, rows, half)).reshape(half, half)
    spread = jnp.where(same, spread, 0.0)
    for part in range(PARTS):
        mixed[part] = dot(spread, slab[part])
        p_v[place(part, me)] = mixed[part, block(me)]
        each_peer(lambda device, index: copy_p(part, device, index, me).start())

    loads[2].wait()
    inverse = 1.0 / scale
    out_v[...] = cross[...] + w_v[...] * inverse
    for part in range(PARTS):
        each_peer(lambda device, index: copy_p(part, device, me, index).wait_recv())
        at = pl.ds(part * half, half)
        arrived = p_v[at, :]
        out_v[...] -= dot(second[:, at], arrived)
        out_v[at, :] -= arrived * (1.0 + inverse)
    store = pltpu.make_async_copy(out_v, out_hbm, out_sem)
    store.start()

    for part in range(PARTS):
        each_peer(lambda device, index: copy_w(part, device, index, me).wait_send())
        each_peer(lambda device, index: copy_p(part, device, index, me).wait_send())
    each_peer(lambda device, index: copy_g(device, index, me).wait_send())
    store.wait()


def fused(sizes, weights, features, targets):
    count = math.prod(sizes)
    feats, beams = weights.shape[1:]
    batch = features.shape[0]
    half = feats // PARTS
    lanes = 128
    f32 = jnp.float32
    any_space = pl.BlockSpec(memory_space=pl.ANY)
    dma = pltpu.SemaphoreType.DMA
    result = pl.pallas_call(
        functools.partial(body, sizes),
        out_shape=jax.ShapeDtypeStruct((feats, beams), f32),
        in_specs=[any_space] * 3,
        out_specs=any_space,
        scratch_shapes=[
            pltpu.VMEM((feats, beams), f32),
            pltpu.VMEM((batch, feats), f32),
            pltpu.VMEM((batch, beams), f32),
            pltpu.VMEM((PARTS, half, beams), f32),
            pltpu.VMEM((PARTS, half, beams), f32),
            pltpu.VMEM((feats, beams), f32),
            pltpu.VMEM((count, lanes), f32),
            pltpu.VMEM((count, count, lanes), f32),
            pltpu.VMEM((feats, feats), f32),
            pltpu.VMEM((feats, beams), f32),
            pltpu.VMEM((feats, beams), f32),
            dma((3 + PARTS,)),
            dma,
            dma((PARTS, count)),
            dma((PARTS, count)),
            dma((count,)),
            dma((count,)),
            dma((PARTS, count)),
            dma((PARTS, count)),
        ],
        compiler_params=pltpu.CompilerParams(
            collective_id=0, has_side_effects=True, vmem_limit_bytes=40 * 1024 * 1024
        ),
    )(weights[0], features, targets)
    return result[None]


def exchanged(sizes, weights, features, targets):
    outer, inner = sizes[0] * sizes[1], sizes[2]
    count = outer * inner
    feats, beams = weights.shape[1:]
    piece = feats * beams // count
    sectioned = weights.reshape(1, outer, inner, piece)
    slab = lax.all_to_all(
        lax.all_to_all(sectioned, AXES[:2], split_axis=1, concat_axis=0, tiled=True),
        AXES[2], split_axis=2, concat_axis=1, tiled=True,
    ).reshape(count, piece)
    gram = lax.psum(dot(slab, slab, ((1,), (1,))), AXES)
    normal, scale = kernel_weights(gram, count, feats * beams)
    back = dot(normal, slab).reshape(outer, inner, 1, 1, piece)
    mean = lax.all_to_all(
        lax.all_to_all(back, AXES[:2], split_axis=0, concat_axis=2, tiled=True),
        AXES[2], split_axis=1, concat_axis=3, tiled=True,
    ).reshape(feats, beams)
    second = dot(features, features, ((0,), (0,)))
    cross = dot(features, targets, ((0,), (0,)))
    return (cross - dot(second, mean) - mean + (weights[0] - mean) / scale)[None]


def solution(mesh):
    sizes = tuple(mesh.shape[name] for name in AXES)
    count = math.prod(sizes)

    def on_device(weights, features, targets):
        feats = weights.shape[1]
        small = count <= 16 and feats % (PARTS * count * 8) == 0
        return (fused if small else exchanged)(sizes, weights, features, targets)

    placed = (
        P(("groups", "particle", "cuts", "sub"), None, None),
        P("groups", None),
        P("groups", None),
    )
    return jax.shard_map(
        on_device,
        mesh=mesh,
        in_specs=placed,
        out_specs=P(("groups", "particle", "cuts", "sub"), None, None),
        check_vma=False,
    )
```

time: 173 us -> 72.1 us (0.42)
  blocking collectives: 73.5 us -> 0 us
  Pallas kernels: 0 us -> 66.5 us
  waiting for transfers between devices: 44.1 us -> 0 us
  local copies, waits for them, and re-layouts: 28.2 us -> 5.38 us
  matrix products: 13.9 us -> 0 us
  starting transfers between devices: 11 us -> 0 us
    pallas_call x0 -> x1, Pallas kernels: none -> 66.5 us  [fused(): pl.pallas_call(functools.partial(body, sizes), out_shape=jax.ShapeDtypeSt...]
    all_to_all x2 -> x0, waiting for transfers between devices: 44.1 us -> none  [the longest x1 24 us: on_device(): lax.all_to_all(grad_sectioned, ('particle', 'cuts'), split_axis=1, concat...]
    all_to_all x4 -> x0, blocking collectives: 41.4 us -> none  [the longest x1 26.9 us: on_device(): lax.all_to_all(back_sectioned, ('particle', 'cuts'), split_axis=0, concat...]
    psum x1 -> x0, blocking collectives: 32.1 us -> none  [kernel_weights(): gram = lax.psum(partial_value, ('particle', 'cuts', 'sub'))]
    dot_general x5 -> x0, matrix products: 13.9 us -> none  [the longest x1 4.58 us: posterior_grad(): lax.dot_general(features, misfit, (((0,), (0,)), ((), ())), precision=hig...]
    reshape x6 -> x0, local copies, waits for them, and re-layouts: 13.6 us -> none  [the longest x1 3.08 us: on_device(): grad_sectioned = grads.reshape(1, outer, inner, piece)]
    all_to_all x2 -> x0, starting transfers between devices: 11 us -> none  [the longest x1 7.26 us: on_device(): lax.all_to_all(grad_sectioned, ('particle', 'cuts'), split_axis=1, concat...]
    all_to_all x6 -> x0, local copies, waits for them, and re-layouts: 8.65 us -> none  [the longest x1 3 us: on_device(): lax.all_to_all(lax.all_to_all(grad_sectioned, ('particle', 'cuts'), split...]
  transfers between devices with their start and end apart: 2 -> 0, of which waited for: 2 -> 0; matrix products, arithmetic and copies ran while one was open for 5% -> 0% of each run, Pallas kernels for 0% -> 0%
where the time goes in v1:
time: 72.1 us; the launch traced here: 71.9 us
  Pallas kernels  66.5 us (92%)
  local copies, waits for them, and re-layouts  5.38 us (7%)
    pallas_call x1, Pallas kernels, fused(): pl.pallas_call(functools.partial(body, sizes), out_shape=jax.ShapeDtypeSt...  66.5 us
    unnamed x7, local copies, waits for them, and re-layouts  5.38 us

profile of v1, /device:TPU:0, one launch (start us, length us, event | category | flops | bytes accessed | tf_op | source)
XLA Modules:
  0.0 71.9 jit_solution(15967136390205822025)
XLA Ops:
  0.0 0.0 copy-start
  0.0 1.6 %copy-done = f32[1024,512]{1,0:T(8,128)S(1)} copy-done((f32[1024,512]{1,0:T(8,128)S(1)}, f32[1024,512]{1,0:T(8,128)}, u32[]{:S(2)}) %copy-start) | copy-done | bytes 2097176
  1.6 0.0 copy-start.1
  1.6 1.6 %copy-done.1 = f32[1024,512]{1,0:T(8,128)S(1)} copy-done((f32[1024,512]{1,0:T(8,128)S(1)}, f32[1024,512]{1,0:T(8,128)}, u32[]{:S(2)}) %copy-start.1) | copy-done | bytes 2097176
  3.2 0.0 copy-start.2
  3.2 1.2 %copy-done.2 = f32[1,512,512]{2,1,0:T(8,128)S(1)} copy-done((f32[1,512,512]{2,1,0:T(8,128)S(1)}, f32[1,512,512]{2,1,0:T(8,128)}, u32[]{:S(2)}) %copy-start.2) | copy-done | bytes 1048600
  4.4 66.5 %shard_map.37 = f32[512,512]{1,0:T(8,128)S(1)} custom-call(f32[512,512]{1,0:T(8,128)S(1)} %bitcast.3, f32[1024,512]{1,0:T(8,128)S(1)} %copy-done, f32[1024,512]{1,0:T(8,128)S(1)} %copy-done.1), custom_call_target="tpu_custom_call" | custom-call | tf_op jit(solution)/shard_map/pallas_call | solution.py:172
  71.0 1.0 %copy.5 = f32[1,512,512]{2,1,0:T(8,128)} copy(f32[1,512,512]{2,1,0:T(8,128)S(1)} %bitcast.2) | data formatting | bytes 2097152
Async XLA Ops:
  0.0 1.6 %copy-start = (f32[1024,512]{1,0:T(8,128)S(1)}, f32[1024,512]{1,0:T(8,128)}, u32[]{:S(2)}) copy-start(f32[1024,512]{1,0:T(8,128)} %x_hbm.1) | copy-start | bytes 6291460
  1.6 1.6 %copy-start.1 = (f32[1024,512]{1,0:T(8,128)S(1)}, f32[1024,512]{1,0:T(8,128)}, u32[]{:S(2)}) copy-start(f32[1024,512]{1,0:T(8,128)} %t_hbm.1) | copy-start | bytes 6291460
  3.2 1.2 %copy-start.2 = (f32[1,512,512]{2,1,0:T(8,128)S(1)}, f32[1,512,512]{2,1,0:T(8,128)}, u32[]{:S(2)}) copy-start(f32[1,512,512]{2,1,0:T(8,128)} %param.3) | copy-start | bytes 3145732

commit v2 on v1

--- a/solution.py
+++ b/solution.py
@@ -44,18 +44,23 @@
     mine = [lax.axis_index(name) for name in AXES]
     me = (mine[0] * n_cuts + mine[1]) * n_sub + mine[2]
 
-    def peer(k):
-        k = count - 1 - k
-        z = lax.rem(mine[0] + k // (n_cuts * n_sub), n_particle)
-        x = lax.rem(mine[1] + lax.rem(k // n_sub, n_cuts), n_cuts)
-        c = lax.rem(mine[2] + lax.rem(k, n_sub), n_sub)
-        return (group, z, x, c), (z * n_cuts + x) * n_sub + c
+    def flipped(position, size, flip):
+        out, bit = 0, 1
+        while bit < size:
+            digit = lax.rem(position // bit, 2)
+            out = out + bit * (1 - digit if flip // bit % 2 else digit)
+            bit *= 2
+        return out
+
+    along = [[flipped(at, size, flip) for flip in range(size)] for at, size in zip(mine, sizes)]
+    peers = [
+        ((group, z, x, c), (z * n_cuts + x) * n_sub + c)
+        for z in along[0] for x in along[1] for c in along[2]
+    ][1:]
 
     def each_peer(step):
-        def go(k, carry):
-            step(*peer(k))
-            return carry
-        lax.fori_loop(0, count - 1, go, 0)
+        for device, index in peers:
+            step(device, index)
 
     def place(part, index):
         return pl.ds(pl.multiple_of(part * half + index * rows, rows), rows)
@@ -121,17 +126,31 @@
         lax.rem(lax.broadcasted_iota(jnp.int32, (half, half), 0), rows)
         == lax.rem(lax.broadcasted_iota(jnp.int32, (half, half), 1), rows)
     )
-    lanes = gram_own.shape[1]
-    total = jnp.where(same, total, 0.0).reshape(count, rows, half)
+    flat = gram_own.shape[1]
+    lanes = 128
+    total = jnp.sum(jnp.where(same, total, 0.0).reshape(count, rows, half), axis=1)
+    to_flat = (
+        lax.broadcasted_iota(jnp.int32, (half, flat), 0) // rows
+        == lax.rem(lax.broadcasted_iota(jnp.int32, (half, flat), 1), count)
+    ).astype(jnp.float32)
+    on_row = (
+        lax.broadcasted_iota(jnp.int32, (count, flat), 1) // count
+        == lax.broadcasted_iota(jnp.int32, (count, flat), 0)
+    )
+    gram_own[...] = jnp.sum(jnp.where(on_row, dot(total, to_flat), 0.0), axis=0, keepdims=True)
+    each_peer(lambda device, index: copy_g(device, index, me).start())
+    gram_all[pl.ds(me, 1)] = gram_own[...][None]
+    each_peer(lambda device, index: copy_g(device, me, index).wait_recv())
+    gram = jnp.where(on_row, jnp.broadcast_to(jnp.sum(gram_all[...], axis=0), (count, flat)), 0.0)
+    from_flat = (
+        lax.rem(lax.broadcasted_iota(jnp.int32, (flat, lanes), 0), count)
+        == lax.broadcasted_iota(jnp.int32, (flat, lanes), 1)
+    ).astype(jnp.float32)
+    gram = dot(gram, from_flat)
     pick = (
         lax.broadcasted_iota(jnp.int32, (half, lanes), 0) // rows
         == lax.broadcasted_iota(jnp.int32, (half, lanes), 1)
     ).astype(jnp.float32)
-    gram_own[...] = dot(jnp.sum(total, axis=1), pick)
-    each_peer(lambda device, index: copy_g(device, index, me).start())
-    gram_all[pl.ds(me, 1)] = gram_own[...][None]
-    each_peer(lambda device, index: copy_g(device, me, index).wait_recv())
-    gram = jnp.sum(gram_all[...], axis=0)
     normal, scale = kernel_weights(gram, count, feats * beams)
     spread = dot(normal, pick, ((1,), (1,)))
     spread = jnp.broadcast_to(spread[:, None, :], (count, rows, half)).reshape(half, half)
@@ -165,7 +184,7 @@
     feats, beams = weights.shape[1:]
     batch = features.shape[0]
     half = feats // PARTS
-    lanes = 128
+    flat = max(count * count, 128)
     f32 = jnp.float32
     any_space = pl.BlockSpec(memory_space=pl.ANY)
     dma = pltpu.SemaphoreType.DMA
@@ -181,8 +200,8 @@
             pltpu.VMEM((PARTS, half, beams), f32),
             pltpu.VMEM((PARTS, half, beams), f32),
             pltpu.VMEM((feats, beams), f32),
-            pltpu.VMEM((count, lanes), f32),
-            pltpu.VMEM((count, count, lanes), f32),
+            pltpu.VMEM((1, flat), f32),
+            pltpu.VMEM((count, 1, flat), f32),
             pltpu.VMEM((feats, feats), f32),
             pltpu.VMEM((feats, beams), f32),
             pltpu.VMEM((feats, beams), f32),
@@ -196,7 +215,7 @@
             dma((PARTS, count)),
         ],
         compiler_params=pltpu.CompilerParams(
-            collective_id=0, has_side_effects=True, vmem_limit_bytes=40 * 1024 * 1024
+            collective_id=0, has_side_effects=True, vmem_limit_bytes=60 * 1024 * 1024
         ),
     )(weights[0], features, targets)
     return result[None]
@@ -231,6 +250,7 @@
     def on_device(weights, features, targets):
         feats = weights.shape[1]
         small = count <= 16 and feats % (PARTS * count * 8) == 0
+        small = small and all(size & (size - 1) == 0 for size in sizes)
         return (fused if small else exchanged)(sizes, weights, features, targets)
 
     placed = (

time: 72.1 us -> 65.4 us (0.907)
  Pallas kernels: 66.5 us -> 62.5 us
  local copies, waits for them, and re-layouts: 5.38 us -> 2.26 us
    pallas_call x1, Pallas kernels: 66.5 us -> 62.5 us  [fused(): pl.pallas_call(functools.partial(body, sizes), out_shape=jax.ShapeDtypeSt...]
    unnamed x7 -> x1, local copies, waits for them, and re-layouts: 5.38 us -> 2.26 us
where the time goes in v2:
time: 65.4 us; the launch traced here: 64.7 us
  Pallas kernels  62.5 us (96%)
  local copies, waits for them, and re-layouts  2.26 us (3%)
    pallas_call x1, Pallas kernels, fused(): pl.pallas_call(functools.partial(body, sizes), out_shape=jax.ShapeDtypeSt...  62.5 us
    unnamed x1, local copies, waits for them, and re-layouts  2.26 us

profile of v2, /device:TPU:0, one launch (start us, length us, event | category | flops | bytes accessed | tf_op | source)
XLA Modules:
  0.0 64.7 jit_solution(198990225729708697)
XLA Ops:
  0.0 62.5 %shard_map.37 = f32[512,512]{1,0:T(8,128)} custom-call(f32[512,512]{1,0:T(8,128)} %bitcast.3, f32[1024,512]{1,0:T(8,128)} %x_hbm.1, f32[1024,512]{1,0:T(8,128)} %t_hbm.1), custom_call_target="tpu_custom_call" | custom-call | tf_op jit(solution)/shard_map/pallas_call | solution.py:191
  62.5 2.3 %copy.5 = f32[1,512,512]{2,1,0:T(8,128)} copy(f32[1,512,512]{2,1,0:T(8,128)} %bitcast.2) | data formatting | bytes 2097152

commit v3 on v2

--- a/solution.py
+++ b/solution.py
@@ -18,6 +18,18 @@
     return lax.dot_general(
         a, b, (contract, ((), ())), precision=HIGHEST, preferred_element_type=jnp.float32
     )
+
+
+def pick_columns(a, chosen):
+    terms, rest = [], a
+    for _ in range(3):
+        terms.append(rest.astype(jnp.bfloat16))
+        rest = rest - terms[-1].astype(jnp.float32)
+    out = jnp.dot(
+        jnp.concatenate(terms, axis=0), chosen.astype(jnp.float32).astype(jnp.bfloat16),
+        preferred_element_type=jnp.float32,
+    ).reshape(3, a.shape[0], chosen.shape[1])
+    return out[0] + (out[1] + out[2])
 
 
 def kernel_weights(gram, count, width):
@@ -32,9 +44,9 @@
     return kernel_mat / jnp.sum(kernel_mat, axis=1, keepdims=True), scale
 
 
-def body(sizes, w_hbm, x_hbm, t_hbm, out_hbm,
-         w_v, x_v, t_v, slab, mixed, p_v, gram_own, gram_all, second, cross, out_v,
-         local_sem, out_sem, send_w, recv_w, send_g, recv_g, send_p, recv_p):
+def body(sizes, w_hbm, x_hbm, t_hbm, out_v,
+         w_v, x_v, t_v, slab, mixed, p_v, gram_own, gram_all, second, cross,
+         local_sem, send_w, recv_w, send_g, recv_g, send_p, recv_p):
     n_particle, n_cuts, n_sub = sizes
     count = n_particle * n_cuts * n_sub
     feats, beams = w_hbm.shape
@@ -132,12 +144,12 @@
     to_flat = (
         lax.broadcasted_iota(jnp.int32, (half, flat), 0) // rows
         == lax.rem(lax.broadcasted_iota(jnp.int32, (half, flat), 1), count)
-    ).astype(jnp.float32)
+    )
     on_row = (
         lax.broadcasted_iota(jnp.int32, (count, flat), 1) // count
         == lax.broadcasted_iota(jnp.int32, (count, flat), 0)
     )
-    gram_own[...] = jnp.sum(jnp.where(on_row, dot(total, to_flat), 0.0), axis=0, keepdims=True)
+    gram_own[...] = jnp.sum(jnp.where(on_row, pick_columns(total, to_flat), 0.0), axis=0, keepdims=True)
     each_peer(lambda device, index: copy_g(device, index, me).start())
     gram_all[pl.ds(me, 1)] = gram_own[...][None]
     each_peer(lambda device, index: copy_g(device, me, index).wait_recv())
@@ -145,14 +157,14 @@
     from_flat = (
         lax.rem(lax.broadcasted_iota(jnp.int32, (flat, lanes), 0), count)
         == lax.broadcasted_iota(jnp.int32, (flat, lanes), 1)
-    ).astype(jnp.float32)
-    gram = dot(gram, from_flat)
-    pick = (
-        lax.broadcasted_iota(jnp.int32, (half, lanes), 0) // rows
-        == lax.broadcasted_iota(jnp.int32, (half, lanes), 1)
-    ).astype(jnp.float32)
+    )
+    gram = pick_columns(gram, from_flat)
+    to_rows = (
+        lax.broadcasted_iota(jnp.int32, (lanes, half), 1) // rows
+        == lax.broadcasted_iota(jnp.int32, (lanes, half), 0)
+    )
     normal, scale = kernel_weights(gram, count, feats * beams)
-    spread = dot(normal, pick, ((1,), (1,)))
+    spread = pick_columns(normal, to_rows)
     spread = jnp.broadcast_to(spread[:, None, :], (count, rows, half)).reshape(half, half)
     spread = jnp.where(same, spread, 0.0)
     for part in range(PARTS):
@@ -169,14 +181,11 @@
         arrived = p_v[at, :]
         out_v[...] -= dot(second[:, at], arrived)
         out_v[at, :] -= arrived * (1.0 + inverse)
-    store = pltpu.make_async_copy(out_v, out_hbm, out_sem)
-    store.start()
 
     for part in range(PARTS):
         each_peer(lambda device, index: copy_w(part, device, index, me).wait_send())
         each_peer(lambda device, index: copy_p(part, device, index, me).wait_send())
     each_peer(lambda device, index: copy_g(device, index, me).wait_send())
-    store.wait()
 
 
 def fused(sizes, weights, features, targets):
@@ -186,13 +195,12 @@
     half = feats // PARTS
     flat = max(count * count, 128)
     f32 = jnp.float32
-    any_space = pl.BlockSpec(memory_space=pl.ANY)
     dma = pltpu.SemaphoreType.DMA
     result = pl.pallas_call(
         functools.partial(body, sizes),
         out_shape=jax.ShapeDtypeStruct((feats, beams), f32),
-        in_specs=[any_space] * 3,
-        out_specs=any_space,
+        in_specs=[pl.BlockSpec(memory_space=pltpu.HBM)] * 3,
+        out_specs=pl.BlockSpec(memory_space=pltpu.VMEM),
         scratch_shapes=[
             pltpu.VMEM((feats, beams), f32),
             pltpu.VMEM((batch, feats), f32),
@@ -204,9 +212,7 @@
             pltpu.VMEM((count, 1, flat), f32),
             pltpu.VMEM((feats, feats), f32),
             pltpu.VMEM((feats, beams), f32),
-            pltpu.VMEM((feats, beams), f32),
             dma((3 + PARTS,)),
-            dma,
             dma((PARTS, count)),
             dma((PARTS, count)),
             dma((count,)),
@@ -215,7 +221,7 @@
             dma((PARTS, count)),
         ],
         compiler_params=pltpu.CompilerParams(
-            collective_id=0, has_side_effects=True, vmem_limit_bytes=60 * 1024 * 1024
+            collective_id=0, has_side_effects=True, vmem_limit_bytes=52 * 1024 * 1024
         ),
     )(weights[0], features, targets)
     return result[None]

time: 65.4 us -> 62.8 us (0.960)
  Pallas kernels: 62.5 us -> 61.2 us
  local copies, waits for them, and re-layouts: 2.26 us -> 0.97 us
    unnamed x1, local copies, waits for them, and re-layouts: 2.26 us -> 0.97 us
    pallas_call x1, Pallas kernels: 62.5 us -> 61.2 us  [fused(): pl.pallas_call(functools.partial(body, sizes), out_shape=jax.ShapeDtypeSt...]
where the time goes in v3:
time: 62.8 us; the launch traced here: 62.2 us
  Pallas kernels  61.2 us (97%)
  local copies, waits for them, and re-layouts  0.97 us (2%)
    pallas_call x1, Pallas kernels, fused(): pl.pallas_call(functools.partial(body, sizes), out_shape=jax.ShapeDtypeSt...  61.2 us

profile of v3, /device:TPU:0, one launch (start us, length us, event | category | flops | bytes accessed | tf_op | source)
XLA Modules:
  0.0 62.2 jit_solution(4871908400794041172)
XLA Ops:
  0.0 61.2 %shard_map.37 = f32[512,512]{1,0:T(8,128)S(1)} custom-call(f32[512,512]{1,0:T(8,128)} %bitcast.3, f32[1024,512]{1,0:T(8,128)} %x_hbm.1, f32[1024,512]{1,0:T(8,128)} %t_hbm.1), custom_call_target="tpu_custom_call" | custom-call | tf_op jit(solution)/shard_map/pallas_call | solution.py:199
  61.2 1.0 %copy.5 = f32[1,512,512]{2,1,0:T(8,128)} copy(f32[1,512,512]{2,1,0:T(8,128)S(1)} %bitcast.2) | data formatting | bytes 2097152

commit v4 on v3

--- a/solution.py
+++ b/solution.py
@@ -169,9 +169,12 @@
     spread = jnp.where(same, spread, 0.0)
     for part in range(PARTS):
         mixed[part] = dot(spread, slab[part])
+        each_peer(lambda device, index: copy_p(part, device, index, me).start())
         p_v[place(part, me)] = mixed[part, block(me)]
-        each_peer(lambda device, index: copy_p(part, device, index, me).start())
-
+
+    for part in range(PARTS):
+        each_peer(lambda device, index: copy_w(part, device, index, me).wait_send())
+    each_peer(lambda device, index: copy_g(device, index, me).wait_send())
     loads[2].wait()
     inverse = 1.0 / scale
     out_v[...] = cross[...] + w_v[...] * inverse
@@ -181,11 +184,7 @@
         arrived = p_v[at, :]
         out_v[...] -= dot(second[:, at], arrived)
         out_v[at, :] -= arrived * (1.0 + inverse)
-
-    for part in range(PARTS):
-        each_peer(lambda device, index: copy_w(part, device, index, me).wait_send())
         each_peer(lambda device, index: copy_p(part, device, index, me).wait_send())
-    each_peer(lambda device, index: copy_g(device, index, me).wait_send())
 
 
 def fused(sizes, weights, features, targets):

time: 62.8 us -> 62.7 us (level)
  no operation moved by 1% of the time
where the time goes in v4:
time: 62.7 us; the launch traced here: 62.1 us
  Pallas kernels  61.1 us (97%)
  local copies, waits for them, and re-layouts  0.97 us (2%)
    pallas_call x1, Pallas kernels, fused(): pl.pallas_call(functools.partial(body, sizes), out_shape=jax.ShapeDtypeSt...  61.1 us

profile of v4, /device:TPU:0, one launch (start us, length us, event | category | flops | bytes accessed | tf_op | source)
XLA Modules:
  0.0 62.1 jit_solution(1347308796105652855)
XLA Ops:
  0.0 61.1 %shard_map.37 = f32[512,512]{1,0:T(8,128)S(1)} custom-call(f32[512,512]{1,0:T(8,128)} %bitcast.3, f32[1024,512]{1,0:T(8,128)} %x_hbm.1, f32[1024,512]{1,0:T(8,128)} %t_hbm.1), custom_call_target="tpu_custom_call" | custom-call | tf_op jit(solution)/shard_map/pallas_call | solution.py:198
  61.1 1.0 %copy.5 = f32[1,512,512]{2,1,0:T(8,128)} copy(f32[1,512,512]{2,1,0:T(8,128)S(1)} %bitcast.2) | data formatting | bytes 2097152

commit v5 on v4

--- a/solution.py
+++ b/solution.py
@@ -18,6 +18,14 @@
     return lax.dot_general(
         a, b, (contract, ((), ())), precision=HIGHEST, preferred_element_type=jnp.float32
     )
+
+
+def split(a):
+    terms = []
+    for _ in range(3):
+        terms.append(a.astype(jnp.bfloat16))
+        a = a - terms[-1].astype(jnp.float32)
+    return terms
 
 
 def pick_columns(a, chosen):
@@ -45,7 +53,7 @@
 
 
 def body(sizes, w_hbm, x_hbm, t_hbm, out_v,
-         w_v, x_v, t_v, slab, mixed, p_v, gram_own, gram_all, second, cross,
+         w_v, x_v, t_v, slab, mixed, p_v, gram_own, gram_all, second, cross, left_terms,
          local_sem, send_w, recv_w, send_g, recv_g, send_p, recv_p):
     n_particle, n_cuts, n_sub = sizes
     count = n_particle * n_cuts * n_sub
@@ -128,6 +136,10 @@
         return carry
     lax.fori_loop(0, feats // tile, moments, 0)
 
+    for part in range(PARTS):
+        a, b, c = split(second[:, pl.ds(part * half, half)])
+        left_terms[part] = jnp.concatenate([a, a, a, b, b, c], axis=1)
+
     total = jnp.zeros((half, half), jnp.float32)
     for part in range(PARTS):
         own[part].wait()
@@ -182,7 +194,9 @@
         each_peer(lambda device, index: copy_p(part, device, me, index).wait_recv())
         at = pl.ds(part * half, half)
         arrived = p_v[at, :]
-        out_v[...] -= dot(second[:, at], arrived)
+        a, b, c = split(arrived)
+        right_terms = jnp.concatenate([a, b, c, a, b, a], axis=0)
+        out_v[...] -= jnp.dot(left_terms[part], right_terms, preferred_element_type=jnp.float32)
         out_v[at, :] -= arrived * (1.0 + inverse)
         each_peer(lambda device, index: copy_p(part, device, index, me).wait_send())
 
@@ -211,6 +225,7 @@
             pltpu.VMEM((count, 1, flat), f32),
             pltpu.VMEM((feats, feats), f32),
             pltpu.VMEM((feats, beams), f32),
+            pltpu.VMEM((PARTS, feats, 6 * half), jnp.bfloat16),
             dma((3 + PARTS,)),
             dma((PARTS, count)),
             dma((PARTS, count)),

time: 62.7 us -> 62.7 us (level)
  no operation moved by 1% of the time
where the time goes in v5:
time: 62.7 us; the launch traced here: 62 us
  Pallas kernels  61.1 us (97%)
  local copies, waits for them, and re-layouts  0.97 us (2%)
    pallas_call x1, Pallas kernels, fused(): pl.pallas_call(functools.partial(body, sizes), out_shape=jax.ShapeDtypeSt...  61.1 us

profile of v5, /device:TPU:0, one launch (start us, length us, event | category | flops | bytes accessed | tf_op | source)
XLA Modules:
  0.0 62.0 jit_solution(17910539484031309677)
XLA Ops:
  0.0 61.1 %shard_map.37 = f32[512,512]{1,0:T(8,128)S(1)} custom-call(f32[512,512]{1,0:T(8,128)} %bitcast.3, f32[1024,512]{1,0:T(8,128)} %x_hbm.1, f32[1024,512]{1,0:T(8,128)} %t_hbm.1), custom_call_target="tpu_custom_call" | custom-call | tf_op jit(solution)/shard_map/pallas_call | solution.py:212
  61.1 1.0 %copy.5 = f32[1,512,512]{2,1,0:T(8,128)} copy(f32[1,512,512]{2,1,0:T(8,128)S(1)} %bitcast.2) | data formatting | bytes 2097152
